TPU v7x, 256 devices: a whole 4x4x8 slice. The times are simulated.
256 devices in a mesh: grp: 4 (over y_lo, core), doc: 16 (over z, y_hi), col: 4 (over x).
Axes of the slice: x: 4, y: 4 (y_hi: 2, y_lo: 2; y = y_hi * 2 + y_lo), z: 8, core: 2. Of those that a mesh axis runs over, the one named last changes fastest.
Arguments:
- mlp_input: bfloat16 [6144, 4096], P('grp', 'col'), may hold values from -6 to 6
- out_grad: bfloat16 [6144, 4096], P('grp', 'col'), may hold values from -6 to 6
- w_gate: bfloat16 [4096, 14336], P('col', 'doc'), may hold values from -0.09375 to 0.09375
- w_up: bfloat16 [4096, 14336], P('col', 'doc'), may hold values from -0.09375 to 0.09375
- w_down: bfloat16 [14336, 4096], P('doc', 'col'), may hold values from -0.046875 to 0.046875
- proj_down_in: bfloat16 [14336, 64], P('doc'), may hold values from -0.046875 to 0.046875
- proj_down_out: bfloat16 [4096, 64], P('col'), may hold values from -0.09375 to 0.09375
- proj_up_in: bfloat16 [4096, 64], P('col'), may hold values from -0.09375 to 0.09375
- proj_up_out: bfloat16 [14336, 64], P('doc'), may hold values from -0.046875 to 0.046875
- store: bfloat16 [32768, 8192], P(('grp', 'doc'), 'col'), may hold values from -100 to 100
- layer_mask: int32 [32768, 2], P(('grp', 'doc')), may hold values 0 or 1
- live_count: int32 [64], P(('grp', 'doc')), may hold values from 1 to 512, 16384 in all
Outputs:
- scores: float32 [24, 32768], P(None, ('grp', 'doc', 'col'))
Inputs may be any that keep to these rules, and one draw needn't show every extreme that they name: Owner p = grp index * 16 + doc index holds slots p * 512 to p * 512 + 511; the first live_count[p] of them hold documents.
All inputs are finite; a program needn't handle non-finite values. No bound on the sum of `layer_mask` or of `live_count` on one device may be relied on, other than what follows from the above.
Results may differ from a plain program's by a relative error of at most 0.03.
Values may be sent and summed in bfloat16 or wider, within the bound.
A program may use at most 128 MiB of HBM per device.

v0:
```python
import math

import jax
import jax.numpy as jnp
from jax import lax
from jax.sharding import PartitionSpec as P

SEQ = 256


epsilon = 1e-06


def fdot(left, right):
    return jnp.dot(left, right, preferred_element_type=jnp.float32)


def local(
    mlp_input,
    out_grad,
    w_gate,
    w_up,
    w_down,
    proj_down_in,
    proj_down_out,
    proj_up_in,
    proj_up_out,
    store,
    layer_mask,
    live_count,
):
    unit_width = w_gate.shape[1]
    token_count = mlp_input.shape[0]
    proj_dim = proj_down_in.shape[1]
    row_share = token_count // lax.axis_size("col")
    summed = lax.psum_scatter(
        jnp.concatenate(
            [
                fdot(mlp_input, w_gate),
                fdot(mlp_input, w_up),
                fdot(out_grad, w_down.T),
                fdot(out_grad, proj_down_out),
                fdot(mlp_input, proj_up_in),
            ],
            axis=1,
        ).astype(jnp.bfloat16),
        "col",
        scatter_dimension=0,
        tiled=True,
    ).astype(jnp.float32)
    gate_value = summed[:, :unit_width]
    up_value = summed[:, unit_width : 2 * unit_width]
    hidden_grad = summed[:, 2 * unit_width : 3 * unit_width]
    down_out = summed[:, 3 * unit_width : 3 * unit_width + proj_dim]
    up_in = summed[:, 3 * unit_width + proj_dim :]
    first_row = lax.axis_index("col") * row_share
    sigmoid_gate = jax.nn.sigmoid(gate_value)
    hidden = (gate_value * sigmoid_gate * up_value).astype(jnp.bfloat16)
    up_grad = (hidden_grad * gate_value * sigmoid_gate).astype(jnp.bfloat16)
    down_in = fdot(hidden, proj_down_in)
    up_out = fdot(up_grad, proj_up_out)
    row_total = down_in.shape[0]
    seq_count = token_count // SEQ
    owner_seq = (first_row + jnp.arange(row_total, dtype=jnp.int32)) // SEQ
    onehot = (owner_seq[None, :] == jnp.arange(seq_count, dtype=jnp.int32)[:, None]).astype(
        jnp.float32
    )
    down_grads = jnp.einsum(
        "qt,tk,tl->qkl", onehot, down_out, down_in, precision=lax.Precision.HIGHEST
    )
    up_grads = jnp.einsum("qt,tk,tl->qkl", onehot, up_out, up_in, precision=lax.Precision.HIGHEST)
    local_query = jnp.concatenate(
        [
            down_grads.reshape(seq_count, proj_dim * proj_dim),
            up_grads.reshape(seq_count, proj_dim * proj_dim),
        ],
        axis=1,
    )
    column_total = local_query.shape[1]
    column_share = store.shape[1]
    padded = jnp.zeros((seq_count * lax.axis_size("grp"), column_total), jnp.float32)
    padded = lax.dynamic_update_slice_in_dim(
        padded, local_query, lax.axis_index("grp") * seq_count, 0
    )
    query_full = lax.psum(padded, ("grp", "doc", "col"))
    square_sums = jnp.sum(query_full * query_full, axis=1)
    query_block = lax.dynamic_slice_in_dim(
        query_full, lax.axis_index("col") * column_share, column_share, 1
    )
    query_unit = (query_block / jnp.sqrt(square_sums / column_total + epsilon)[:, None]).astype(
        jnp.bfloat16
    )
    module_index = lax.axis_index("col") // (lax.axis_size("col") // 2)
    doc_mask = jnp.where(module_index == 0, layer_mask[:, 0], layer_mask[:, 1]).astype(jnp.float32)
    raw_scores = fdot(query_unit, store.T)
    doc_squares = jnp.sum(jnp.square(store.astype(jnp.float32)), axis=1)
    raw_scores, doc_squares = (
        lax.psum_scatter(
            (raw_scores * doc_mask[None, :]).astype(jnp.bfloat16),
            "col",
            scatter_dimension=1,
            tiled=True,
        ).astype(jnp.float32),
        lax.psum_scatter(
            (doc_squares * doc_mask)[None, :].astype(jnp.bfloat16),
            "col",
            scatter_dimension=1,
            tiled=True,
        ).astype(jnp.float32),
    )
    out_width = raw_scores.shape[1]
    slot_index = lax.axis_index("col") * out_width + jnp.arange(out_width, dtype=jnp.int32)
    live_slots = slot_index < live_count[0]
    scaled = raw_scores / (jnp.sqrt(doc_squares / column_total + epsilon) * math.sqrt(column_total))
    return jnp.where(live_slots[None, :], scaled, 0.0)


def solution(mesh):
    return jax.shard_map(
        local,
        mesh=mesh,
        in_specs=(
            P("grp", "col"),
            P("grp", "col"),
            P("col", "doc"),
            P("col", "doc"),
            P("doc", "col"),
            P("doc", None),
            P("col", None),
            P("col", None),
            P("doc", None),
            P(("grp", "doc"), "col"),
            P(("grp", "doc"), None),
            P(("grp", "doc")),
        ),
        out_specs=P(None, ("grp", "doc", "col")),
        check_vma=False,
    )
```

profile of v0, /device:TPU:1, one launch (start us, length us, event | category | flops | bytes accessed | tf_op | source)
XLA Modules:
  0.0 454.0 jit_solution(13002228726567489770)
XLA Ops:
  6.5 1.9 copy-done
  8.4 6.1 %fusion.2 = bf16[1536,2816]{0,1:T(8,128)(2,1)} fusion(bf16[1536,1024]{1,0:T(8,128)(2,1)S(1)} %copy-done, bf16[1024,896]{1,0:T(8,128)(2,1)} %param.14), kind=kOutput, calls=%fused_computation.6 | convolution fusion | flops 2819948544 | bytes 7733248 | tf_op jit(solution)/shard_map/dot_general | solution.py:15
  14.6 4.5 %fusion.1 = bf16[1536,2816]{0,1:T(8,128)(2,1)} fusion(bf16[1536,2816]{0,1:T(8,128)(2,1)} %fusion.2, bf16[1536,1024]{1,0:T(8,128)(2,1)S(1)} %copy-done, bf16[1024,896]{1,0:T(8,128)(2,1)S(1)} %copy-done.6), kind=kOutput, calls=%fused_computation.4 | convolution fusion | flops 2819948544 | bytes 7733248 | tf_op jit(solution)/shard_map/dot_general | solution.py:15
  19.1 4.4 fusion
  23.5 1.8 fusion.4
  25.3 1.8 fusion.3
  27.0 11.7 %copy.13 = bf16[1536,2816]{1,0:T(8,128)(2,1)} copy(bf16[1536,2816]{0,1:T(8,128)(2,1)} %fusion.3) | data formatting | bytes 17301504
  38.9 89.0 %reduce-scatter.10.cloned.1.call-done = bf16[384,2816]{1,0:T(8,128)(2,1)} async-done(((bf16[1536,2816]{1,0:T(8,128)(2,1)}), bf16[384,2816]{1,0:T(8,128)(2,1)}) %reduce-scatter.10.cloned.1.call-update) | async-done | bytes 2162704
  128.0 4.2 copy.14
  132.1 1.9 convert_element_type.56
  134.1 0.9 slice_convert_fusion
  134.9 0.5 convolution_bitcast_fusion.2
  135.5 0.6 copy-done.2
  136.1 0.6 convolution_bitcast_fusion.1
  136.7 0.1 reshape.78
  136.8 2.3 fusion.10
  139.1 1.2 convolution_bitcast_fusion
  140.3 0.8 reshape.79
  141.1 0.9 pad_maximum_fusion
  142.0 1.0 broadcast_in_dim.22
  143.0 1.8 dynamic_update_slice.3
  144.8 2.1 multiply_reduce_fusion
  146.9 0.8 copy.17
  148.5 248.9 %all-reduce.2.cloned.1.call-done = f32[24,8192]{1,0:T(8,128)} async-done(((f32[24,8192]{1,0:T(8,128)}), f32[24,8192]{1,0:T(8,128)}) %all-reduce.2.cloned.1.call-update) | async-done | bytes 786448 | tf_op jit(solution)/shard_map/psum | solution.py:85
  397.4 1.3 multiply_reduce_fusion.1
  398.7 2.4 fusion.8
  401.1 0.8 copy.15
  401.9 19.1 %reduce-scatter.14.cloned.1.call-done = bf16[128,1]{1,0:T(8,128)(2,1)} async-done(((bf16[512,1]{1,0:T(8,128)(2,1)}), bf16[128,1]{1,0:T(8,128)(2,1)}) %reduce-scatter.14.cloned.1.call-update) | async-done | bytes 272
  420.9 0.8 multiply_bitcast_fusion
  421.8 24.2 %reduce-scatter.12.cloned.1.call-done = bf16[128,24]{1,0:T(8,128)(2,1)} async-done(((bf16[512,24]{1,0:T(8,128)(2,1)}), bf16[128,24]{1,0:T(8,128)(2,1)}) %reduce-scatter.12.cloned.1.call-update) | async-done | bytes 6160
  446.0 0.8 copy.16
  446.8 0.6 divide_select_fusion
  (30 shorter events, 0.3 us)
Async XLA Ops:
  6.5 1.9 copy-start
  6.5 121.4 %reduce-scatter.10.cloned.1.call-start = ((), (), s32[]{:S(2)}) async-start(), calls=%async_computation.4 | async-start | bytes 10813440
  8.4 6.2 %copy-start.6 = (bf16[1024,896]{1,0:T(8,128)(2,1)S(1)}, bf16[1024,896]{1,0:T(8,128)(2,1)}, u32[]{:S(2)}) copy-start(bf16[1024,896]{1,0:T(8,128)(2,1)} %param.15) | copy-start | bytes 5505028
  14.6 4.6 %copy-start.1 = (bf16[1536,1024]{1,0:T(8,128)(2,1)S(1)}, bf16[1536,1024]{1,0:T(8,128)(2,1)}, u32[]{:S(2)}) copy-start(bf16[1536,1024]{1,0:T(8,128)(2,1)} %param.13) | copy-start | bytes 9437188
  14.6 4.6 %copy-start.7 = (bf16[896,1024]{1,0:T(8,128)(2,1)S(1)}, bf16[896,1024]{1,0:T(8,128)(2,1)}, u32[]{:S(2)}) copy-start(bf16[896,1024]{1,0:T(8,128)(2,1)} %param.16) | copy-start | bytes 5505028
  19.1 4.4 copy-start.3
  23.5 1.8 copy-start.4
  38.8 358.6 %all-reduce.2.cloned.1.call-start = ((), (), s32[]{:S(2)}) async-start(), calls=%async_computation.3 | async-start | bytes 1572864 | tf_op jit(solution)/shard_map/psum | solution.py:85
  132.1 2.8 copy-start.8
  134.1 2.0 copy-start.2
  139.1 7.8 %copy-start.5 = (s32[512,2]{0,1:T(2,128)S(1)}, s32[512,2]{0,1:T(2,128)}, u32[]{:S(2)}) copy-start(s32[512,2]{0,1:T(2,128)} %param.22) | copy-start | bytes 12292
  144.8 276.2 %reduce-scatter.14.cloned.1.call-start = ((), (), s32[]{:S(2)}) async-start(), calls=%async_computation.6 | async-start | bytes 163840
  147.8 298.2 %reduce-scatter.12.cloned.1.call-start = ((), (), s32[]{:S(2)}) async-start(), calls=%async_computation.5 | async-start | bytes 163840
Sparse Core Ops, SparseCore 0:
  38.9 88.9 reduce-scatter.9
  144.9 252.4 all-reduce.1
  400.0 20.8 reduce-scatter.13
  423.3 22.6 reduce-scatter.11
where the time goes:
time: 456 us; the launch traced here: 454 us
  waiting for transfers between devices  381 us (84%)
  matrix products  25.6 us (6%)
  local copies, waits for them, and re-layouts  24.5 us (5%)
  between operations  13.9 us (3%)
  other arithmetic  8.56 us (2%)
    psum x1, waiting for transfers between devices, local(): query_full = lax.psum(padded, ('grp', 'doc', 'col'))  249 us
    unnamed x7, waiting for transfers between devices  132 us
    dot_general x8, matrix products, fdot(): return jnp.dot(left, right, preferred_element_type=jnp.float32)  23.8 us
    unnamed x24, local copies, waits for them, and re-layouts  20.9 us
  transfers between devices with their start and end apart: 4, of which 4 were waited for; matrix products, arithmetic and copies ran while one was open for 2% of the time, Pallas kernels for 0%

commit v1 on v0

v1 whole, which is shorter than its diff:
```python
import functools
import math

import jax
import jax.numpy as jnp
from jax import lax
from jax.experimental import pallas as pl
from jax.experimental.pallas import tpu as pltpu
from jax.sharding import PartitionSpec as P

MESH = pl.DeviceIdType.MESH
SEQ = 256
LANES = 128
EPSILON = 1e-06
NT = (((1,), (1,)), ((), ()))
f32, bf16 = jnp.float32, jnp.bfloat16


def dot(left, right):
    return jnp.dot(left, right, preferred_element_type=f32)


def dot_nt(left, right):
    return lax.dot_general(left, right, NT, preferred_element_type=f32)


def kernel(
    sizes,
    x_in,
    og_in,
    wg_in,
    wu_in,
    wd_in,
    pdi_in,
    pdo_in,
    pui_in,
    puo_in,
    store_in,
    mask_in,
    out_ref,
    x,
    og,
    wg,
    wu,
    wd,
    pdi,
    pdo,
    pui,
    puo,
    store,
    mask,
    gate,
    up,
    hg,
    s,
    send_a,
    recv_a,
    send_b,
    recv_b,
    ends_part,
    ends_recv,
    ends,
    ends_t,
    ui2,
    pairs,
    grads,
    x_recv,
    block,
    d_recv,
    full,
    select,
    c_send,
    c_recv,
    load_sem,
    ring_s,
    ring_r,
    ends_s,
    ends_r,
    gather_s,
    gather_r,
    x_s,
    x_r,
    d1_s,
    d1_r,
    d2_s,
    d2_r,
    g_s,
    g_r,
    c_s,
    c_r,
):
    n_grp, n_doc, n_col, nq = sizes
    part = SEQ // n_col
    half = part // 2
    g, d, c = lax.axis_index("grp"), lax.axis_index("doc"), lax.axis_index("col")
    right, left, across = (
        lax.rem(c + 1, n_col),
        lax.rem(c + n_col - 1, n_col),
        lax.rem(c + 2, n_col),
    )

    def remote(src, dst, send, recv, **place):
        return pltpu.make_async_remote_copy(
            src_ref=src,
            dst_ref=dst,
            send_sem=send,
            recv_sem=recv,
            device_id=place,
            device_id_type=MESH,
        )

    loads = {}

    def load(key, src, dst):
        copy = pltpu.make_async_copy(src, dst, load_sem.at[len(loads)])
        copy.start()
        loads[key] = copy

    load("wg", wg_in, wg)
    load("x", x_in, x)
    load("wu", wu_in, wu)
    load("og", og_in, og)
    load("wd", wd_in, wd)
    k_dim = pdi_in.shape[0]
    load("pdo", pdo_in, pdo.at[pl.ds(0, k_dim)])
    load("pui", pui_in, pui.at[pl.ds(k_dim, k_dim)])
    load("pdi", pdi_in, pdi.at[pl.ds(0, k_dim)])
    load("pdi2", pdi_in, pdi.at[pl.ds(k_dim, k_dim)])
    load("puo", puo_in, puo)
    load("store", store_in, store)
    load("mask", mask_in, mask)

    barrier = pltpu.get_barrier_semaphore()
    for k in range(1, n_col):
        pl.semaphore_signal(
            barrier, 1, device_id={"col": lax.rem(c + k, n_col)}, device_id_type=MESH
        )
    for k in range(1, n_grp):
        pl.semaphore_signal(
            barrier, 1, device_id={"grp": lax.rem(g + k, n_grp)}, device_id_type=MESH
        )

    def greet(k, carry):
        pl.semaphore_signal(
            barrier, 1, device_id={"doc": lax.rem(d + k, n_doc)}, device_id_type=MESH
        )
        return carry

    lax.fori_loop(1, n_doc, greet, 0)
    pl.semaphore_wait(barrier, n_col + n_grp + n_doc - 3)

    def copy_a(p, way):
        rows = pl.ds(way * half, half)
        return remote(
            send_a.at[p, rows],
            recv_a.at[p, way],
            ring_s.at[0, p, way],
            ring_r.at[0, p, way],
            col=(right, left)[way],
        )

    def copy_b(p, way):
        return remote(
            send_b.at[p, way],
            recv_b.at[p, way],
            ring_s.at[1, p, way],
            ring_r.at[1, p, way],
            col=(right, left)[way],
        )

    def copy_g(p, way, slot):
        return remote(
            s.at[p, slot],
            s.at[p, slot],
            ring_s.at[2, p, way],
            ring_r.at[2, p, way],
            col=(right, left)[way],
        )

    def copy_f(p, way, slot):
        rows = pl.ds(way * half, half)
        return remote(
            s.at[p, slot, rows],
            s.at[p, slot, rows],
            ring_s.at[3, p, way],
            ring_r.at[3, p, way],
            col=(right, left)[way],
        )

    def token_rows(p):
        return pl.ds(pl.multiple_of(p * SEQ, SEQ), SEQ)

    def own_rows(owner, first, count):
        return pl.ds(pl.multiple_of(owner * part + first, half), count)

    loads["wg"].wait()
    loads["x"].wait()

    def gate_step(p, carry):
        gate[p] = dot(x[token_rows(p)], wg[...])
        send_a[p] = gate[p, own_rows(across, 0, part)].astype(bf16)
        copy_a(p, 0).start()
        copy_a(p, 1).start()
        return carry

    lax.fori_loop(0, nq, gate_step, 0)

    loads["wu"].wait()
    loads["og"].wait()
    loads["wd"].wait()

    def terms_step(p, carry):
        up[p] = dot(x[token_rows(p)], wu[...]).astype(bf16)
        copy_a(p, 0).wait_recv()
        send_b[p, 0, pl.ds(0, half)] = (
            gate[p, own_rows(right, 0, half)] + recv_a[p, 0].astype(f32)
        ).astype(bf16)
        send_b[p, 0, pl.ds(half, half)] = gate[p, own_rows(right, half, half)].astype(bf16)
        copy_b(p, 0).start()
        copy_a(p, 1).wait_recv()
        send_b[p, 1, pl.ds(0, half)] = gate[p, own_rows(left, 0, half)].astype(bf16)
        send_b[p, 1, pl.ds(half, half)] = (
            gate[p, own_rows(left, half, half)] + recv_a[p, 1].astype(f32)
        ).astype(bf16)
        copy_b(p, 1).start()
        hg[p] = dot_nt(og[token_rows(p)], wd[...]).astype(bf16)
        return carry

    lax.fori_loop(0, nq, terms_step, 0)

    slab = ends_part.shape[0]
    loads["pdo"].wait()
    loads["pui"].wait()
    pdo[pl.ds(k_dim, k_dim)] = jnp.zeros((k_dim, pdo.shape[1]), bf16)
    pui[pl.ds(0, k_dim)] = jnp.zeros((k_dim, pui.shape[1]), bf16)
    mine = pl.ds(pl.multiple_of(d * slab, slab), slab)
    ends_part[...] = (dot_nt(og[mine], pdo[...]) + dot_nt(x[mine], pui[...])).astype(bf16)

    def copy_ends(k):
        return remote(
            ends_part,
            ends_recv.at[k - 1],
            ends_s.at[k - 1],
            ends_r.at[k - 1],
            col=lax.rem(c + k, n_col),
        )

    for k in range(1, n_col):
        copy_ends(k).start()

    loads["store"].wait()
    squares = jnp.zeros((store.shape[0], LANES), f32)
    for j in range(store.shape[1] // LANES):
        value = store[:, pl.ds(j * LANES, LANES)].astype(f32)
        squares += value * value
    upper = squares.astype(bf16)
    lower = (squares - upper.astype(f32)).astype(bf16)
    ones = jnp.ones((8, LANES), bf16)
    doc_squares = dot_nt(ones, upper) + dot_nt(ones, lower)
    loads["mask"].wait()
    keep = jnp.where(c < n_col // 2, mask[0:1, :], mask[1:2, :]).astype(f32)
    doc_squares = doc_squares * keep
    out_width = store.shape[0] // n_col
    for j in range(n_col):
        c_send[j, pl.ds(32, 8)] = doc_squares[:, j * out_width : (j + 1) * out_width]

    q_pad = n_doc // 2
    n_pad = q_pad * n_grp
    n_sub = full.shape[0] * full.shape[1] * 8 // n_pad
    row = lax.broadcasted_iota(jnp.int32, (n_pad, n_pad * n_sub), 0)
    lane = lax.broadcasted_iota(jnp.int32, (n_pad, n_pad * n_sub), 1)
    for kk in range(n_sub):
        select[pl.ds(kk * n_pad, n_pad)] = jnp.where(lane == row * n_sub + kk, 1.0, 0.0).astype(
            bf16
        )

    for k in range(1, n_col):
        copy_ends(k).wait_recv()
    total = ends_part[...].astype(f32)
    for k in range(1, n_col):
        total += ends_recv[k - 1].astype(f32)
    ends[mine] = total.astype(bf16)

    def copy_gather(k, owner):
        rows = pl.ds(pl.multiple_of(owner * slab, slab), slab)
        return remote(
            ends.at[rows],
            ends.at[rows],
            gather_s.at[k - 1],
            gather_r.at[k - 1],
            doc=lax.rem(d + k, n_doc),
        )

    def gather_start(k, carry):
        copy_gather(k, d).start()
        return carry

    lax.fori_loop(1, n_doc, gather_start, 0)

    def own_step(p, carry):
        copy_b(p, 0).wait_recv()
        copy_b(p, 1).wait_recv()
        value = (
            gate[p, own_rows(c, 0, part)] + recv_b[p, 0].astype(f32) + recv_b[p, 1].astype(f32)
        )
        s[p, c] = (value * jax.nn.sigmoid(value)).astype(bf16)
        copy_g(p, 0, c).start()
        copy_g(p, 1, c).start()
        return carry

    lax.fori_loop(0, nq, own_step, 0)

    def gather_wait(k, carry):
        copy_gather(k, lax.rem(d + n_doc - k, n_doc)).wait_recv()
        return carry

    lax.fori_loop(1, n_doc, gather_wait, 0)
    low_lanes = lax.broadcasted_iota(jnp.int32, (SEQ, LANES), 1) < k_dim

    def ends_step(p, carry):
        value = ends[token_rows(p)].astype(f32)
        ends_t[p] = value.T[:k_dim].astype(bf16)
        ui2[p] = jnp.where(low_lanes, pltpu.roll(value, k_dim, 1), value).astype(bf16)
        return carry

    lax.fori_loop(0, nq, ends_step, 0)

    def forward_step(p, carry):
        copy_g(p, 0, left).wait_recv()
        copy_f(p, 0, left).start()
        copy_g(p, 1, right).wait_recv()
        copy_f(p, 1, right).start()
        return carry

    lax.fori_loop(0, nq, forward_step, 0)

    loads["pdi"].wait()
    loads["pdi2"].wait()
    loads["puo"].wait()
    for p in range(nq, q_pad):
        grads[p] = jnp.zeros(grads.shape[1:], f32)
    low_half = lax.broadcasted_iota(jnp.int32, (k_dim // 2, LANES), 1) < k_dim

    def grads_step(p, carry):
        copy_f(p, 0, across).wait_recv()
        copy_f(p, 1, across).wait_recv()
        shared = s[p].reshape(SEQ, s.shape[-1])
        down_in = dot_nt(up[p] * shared, pdi[...])
        up_out = dot_nt(puo[...], hg[p] * shared)
        pairs[pl.ds(0, k_dim)] = dot(ends_t[p], down_in.astype(bf16))
        pairs[pl.ds(k_dim, k_dim)] = dot(up_out.astype(bf16), ui2[p])
        for m in range(2):
            even = pairs[pl.ds(m * k_dim, k_dim // 2, 2)]
            odd = pairs[pl.ds(m * k_dim + 1, k_dim // 2, 2)]
            grads[p, pl.ds(m * (k_dim // 2), k_dim // 2)] = jnp.where(low_half, even, odd)
        return carry

    lax.fori_loop(0, nq, grads_step, 0)

    def copy_x(k):
        to = lax.rem(c + k, n_col)
        return remote(
            grads.at[:, pl.ds(pl.multiple_of(to * n_sub, n_sub), n_sub)],
            x_recv.at[k - 1],
            x_s.at[k - 1],
            x_r.at[k - 1],
            col=to,
        )

    for k in range(1, n_col):
        copy_x(k).start()
    for k in range(1, n_col):
        copy_x(k).wait_recv()
    total = grads[:, pl.ds(pl.multiple_of(c * n_sub, n_sub), n_sub)]
    for k in range(1, n_col):
        total += x_recv[k - 1]
    block[...] = total.reshape(block.shape)

    def copy_d1(k):
        to = lax.rem(d + k, n_doc)
        return remote(block.at[to], d_recv.at[k - 1], d1_s.at[k - 1], d1_r.at[k - 1], doc=to)

    def d1_start(k, carry):
        copy_d1(k).start()
        return carry

    lax.fori_loop(1, n_doc, d1_start, 0)

    def d1_wait(k, carry):
        copy_d1(k).wait_recv()
        return carry

    lax.fori_loop(1, n_doc, d1_wait, 0)
    total = block[d]
    for k in range(1, n_doc):
        total += d_recv[k - 1]
    full[g, d] = total

    def copy_d2(k, owner):
        return remote(
            full.at[g, owner],
            full.at[g, owner],
            d2_s.at[k - 1],
            d2_r.at[k - 1],
            doc=lax.rem(d + k, n_doc),
        )

    def d2_start(k, carry):
        copy_d2(k, d).start()
        return carry

    lax.fori_loop(1, n_doc, d2_start, 0)

    def d2_wait(k, carry):
        copy_d2(k, lax.rem(d + n_doc - k, n_doc)).wait_recv()
        return carry

    lax.fori_loop(1, n_doc, d2_wait, 0)

    def copy_grp(k, owner):
        return remote(
            full.at[owner],
            full.at[owner],
            g_s.at[k - 1],
            g_r.at[k - 1],
            grp=lax.rem(g + k, n_grp),
        )

    for k in range(1, n_grp):
        copy_grp(k, g).start()
    for k in range(1, n_grp):
        copy_grp(k, lax.rem(g + n_grp - k, n_grp)).wait_recv()

    ordered = dot(select[...], full[...].reshape(n_pad * n_sub, LANES).astype(bf16))
    query = jnp.concatenate([ordered[kk * n_pad : (kk + 1) * n_pad] for kk in range(n_sub)], axis=1)
    raw = dot_nt(query.astype(bf16), store[...]) * keep
    query_squares = jnp.broadcast_to(
        jnp.sum(query * query, axis=1, keepdims=True), (n_pad, out_width)
    )
    for j in range(n_col):
        c_send[j, pl.ds(0, 32)] = raw[:, j * out_width : (j + 1) * out_width]
        c_send[j, pl.ds(40, 32)] = query_squares

    def copy_c(k):
        to = lax.rem(c + k, n_col)
        return remote(c_send.at[to], c_recv.at[k - 1], c_s.at[k - 1], c_r.at[k - 1], col=to)

    for k in range(1, n_col):
        copy_c(k).start()
    for k in range(1, n_col):
        copy_c(k).wait_recv()
    total = c_send[c]
    for k in range(1, n_col):
        total += c_recv[k - 1]
    columns = float(n_col * n_sub * LANES)
    query_norm = jnp.sqrt(total[40:72] / columns + EPSILON)
    doc_norm = jnp.sqrt(total[32:33] / columns + EPSILON) * math.sqrt(columns)
    out_ref[...] = total[0:32] / (query_norm * doc_norm)

    def ring_done(p, carry):
        for way in range(2):
            copy_a(p, way).wait_send()
            copy_b(p, way).wait_send()
            copy_g(p, way, c).wait_send()
            copy_f(p, way, left).wait_send()
        return carry

    lax.fori_loop(0, nq, ring_done, 0)

    def doc_done(k, carry):
        copy_gather(k, d).wait_send()
        copy_d1(k).wait_send()
        copy_d2(k, d).wait_send()
        return carry

    lax.fori_loop(1, n_doc, doc_done, 0)
    for k in range(1, n_col):
        copy_ends(k).wait_send()
        copy_x(k).wait_send()
        copy_c(k).wait_send()
    for k in range(1, n_grp):
        copy_grp(k, g).wait_send()


def local(
    mlp_input,
    out_grad,
    w_gate,
    w_up,
    w_down,
    proj_down_in,
    proj_down_out,
    proj_up_in,
    proj_up_out,
    store,
    layer_mask,
    live_count,
):
    n_grp, n_doc, n_col = (lax.axis_size(name) for name in ("grp", "doc", "col"))
    tokens, depth = mlp_input.shape
    width = w_gate.shape[1]
    k_dim = proj_down_in.shape[1]
    nq = tokens // SEQ
    q_pad = n_doc // 2
    n_pad = q_pad * n_grp
    part = SEQ // n_col
    slab = tokens // n_doc
    n_row = 2 * k_dim * k_dim // LANES
    n_sub = n_row // n_col
    dma = pltpu.SemaphoreType.DMA
    scratch = [
        pltpu.VMEM((tokens, depth), bf16),
        pltpu.VMEM((tokens, depth), bf16),
        pltpu.VMEM((depth, width), bf16),
        pltpu.VMEM((depth, width), bf16),
        pltpu.VMEM((width, depth), bf16),
        pltpu.VMEM((2 * k_dim, width), bf16),
        pltpu.VMEM((2 * k_dim, depth), bf16),
        pltpu.VMEM((2 * k_dim, depth), bf16),
        pltpu.VMEM((k_dim, width), bf16),
        pltpu.VMEM(store.shape, bf16),
        pltpu.VMEM(layer_mask.shape[::-1], jnp.int32),
        pltpu.VMEM((nq, SEQ, width), f32),
        pltpu.VMEM((nq, SEQ, width), bf16),
        pltpu.VMEM((nq, SEQ, width), bf16),
        pltpu.VMEM((nq, n_col, part, width), bf16),
        pltpu.VMEM((nq, part, width), bf16),
        pltpu.VMEM((nq, 2, part // 2, width), bf16),
        pltpu.VMEM((nq, 2, part, width), bf16),
        pltpu.VMEM((nq, 2, part, width), bf16),
        pltpu.VMEM((slab, LANES), bf16),
        pltpu.VMEM((n_col - 1, slab, LANES), bf16),
        pltpu.VMEM((tokens, LANES), bf16),
        pltpu.VMEM((nq, k_dim, SEQ), bf16),
        pltpu.VMEM((nq, SEQ, LANES), bf16),
        pltpu.VMEM((2 * k_dim, LANES), f32),
        pltpu.VMEM((q_pad, n_row, LANES), f32),
        pltpu.VMEM((n_col - 1, q_pad, n_sub, LANES), f32),
        pltpu.VMEM((n_doc, 8, LANES), f32),
        pltpu.VMEM((n_doc - 1, 8, LANES), f32),
        pltpu.VMEM((n_grp, n_doc, 8, LANES), f32),
        pltpu.VMEM((n_pad * n_sub, n_pad * n_sub), bf16),
        pltpu.VMEM((n_col, 72, store.shape[0] // n_col), f32),
        pltpu.VMEM((n_col - 1, 72, store.shape[0] // n_col), f32),
        dma((12,)),
        dma((4, nq, 2)),
        dma((4, nq, 2)),
        dma((n_col - 1,)),
        dma((n_col - 1,)),
        dma((n_doc - 1,)),
        dma((n_doc - 1,)),
        dma((n_col - 1,)),
        dma((n_col - 1,)),
        dma((n_doc - 1,)),
        dma((n_doc - 1,)),
        dma((n_doc - 1,)),
        dma((n_doc - 1,)),
        dma((n_grp - 1,)),
        dma((n_grp - 1,)),
        dma((n_col - 1,)),
        dma((n_col - 1,)),
    ]
    out_width = store.shape[0] // n_col
    scores = pl.pallas_call(
        functools.partial(kernel, (n_grp, n_doc, n_col, nq)),
        out_shape=jax.ShapeDtypeStruct((n_pad, out_width), f32),
        in_specs=[pl.BlockSpec(memory_space=pl.ANY)] * 11,
        out_specs=pl.BlockSpec(memory_space=pltpu.VMEM),
        scratch_shapes=scratch,
        compiler_params=pltpu.CompilerParams(
            collective_id=0, has_side_effects=True, vmem_limit_bytes=58 * 1024 * 1024
        ),
        cost_estimate=pl.CostEstimate(
            flops=6 * tokens * depth * width, bytes_accessed=14 << 20, transcendentals=0
        ),
    )(
        mlp_input,
        out_grad,
        w_gate,
        w_up,
        w_down,
        proj_down_in.T,
        proj_down_out.T,
        proj_up_in.T,
        proj_up_out.T,
        store,
        layer_mask.T,
    )
    scores = scores.reshape(n_grp, q_pad, out_width)[:, :nq].reshape(n_grp * nq, out_width)
    slot = lax.axis_index("col") * out_width + jnp.arange(out_width, dtype=jnp.int32)
    return jnp.where((slot < live_count[0])[None, :], scores, 0.0)


def solution(mesh):
    return jax.shard_map(
        local,
        mesh=mesh,
        in_specs=(
            P("grp", "col"),
            P("grp", "col"),
            P("col", "doc"),
            P("col", "doc"),
            P("doc", "col"),
            P("doc", None),
            P("col", None),
            P("col", None),
            P("doc", None),
            P(("grp", "doc"), "col"),
            P(("grp", "doc"), None),
            P(("grp", "doc")),
        ),
        out_specs=P(None, ("grp", "doc", "col")),
        check_vma=False,
    )
```

time: 456 us -> 93.4 us (0.20)
  waiting for transfers between devices: 381 us -> 0 us
  Pallas kernels: 0 us -> 91.2 us
  matrix products: 25.6 us -> 0 us
  local copies, waits for them, and re-layouts: 24.5 us -> 0.72 us
  between operations: 13.9 us -> 0.67 us
  other arithmetic: 8.56 us -> 0.61 us
    psum x1 -> x0, waiting for transfers between devices: 249 us -> none  [local(): query_full = lax.psum(padded, ('grp', 'doc', 'col'))]
    unnamed x7 -> x0, waiting for transfers between devices: 132 us -> none
    pallas_call x0 -> x1, Pallas kernels: none -> 91.2 us  [local(): pl.pallas_call(functools.partial(kernel, (n_grp, n_doc, n_col, nq)), out_...]
    dot_general x10 -> x0, matrix products: 25.6 us -> none  [the longest x8 23.8 us: fdot(): return jnp.dot(left, right, preferred_element_type=jnp.float32)]
    unnamed x24 -> x0, local copies, waits for them, and re-layouts: 20.9 us -> none
  transfers between devices with their start and end apart: 4 -> 0, of which waited for: 4 -> 0; matrix products, arithmetic and copies ran while one was open for 2% -> 0% of each run, Pallas kernels for 0% -> 0%
where the time goes in v1:
time: 93.4 us; the launch traced here: 93.2 us
  Pallas kernels  91.2 us (98%)
    pallas_call x1, Pallas kernels, local(): pl.pallas_call(functools.partial(kernel, (n_grp, n_doc, n_col, nq)), out_...  91.2 us

profile of v1, /device:TPU:1, one launch (start us, length us, event | category | flops | bytes accessed | tf_op | source)
XLA Modules:
  0.0 93.2 jit_solution(17374043434517852845)
XLA Ops:
  0.0 91.2 %shard_map.118 = f32[32,128]{1,0:T(8,128)} custom-call(bf16[1536,1024]{1,0:T(8,128)(2,1)} %x_in.1, bf16[1536,1024]{1,0:T(8,128)(2,1)} %og_in.1, bf16[1024,896]{1,0:T(8,128)(2,1)} %wg_in.1, bf16[1024,896]{1,0:T(8,128)(2,1)} %wu_in.1, bf16[896,1024]{1,0:T(8,128)(2,1)} %wd_in.1, bf16[64,896]{1,0:T(8,128)(2,1)} %bitcast.12, bf16[64,1024]{1,0:T(8,128)(2,1)} %bitcast.10, ...), custom_call_target="tpu_custom_call" | custom-call | flops 8455716864 | bytes 14680064 | tf_op jit(solution)/shard_map/pallas_call | solution.py:564
  91.2 0.7 reshape.12
  92.6 0.6 broadcast_select_fusion
  (1 shorter events, 0.0 us)
